TPU v7x, 1024 devices: a whole 4x8x16 slice. The times are simulated.
1024 devices in a mesh: ev: 16 (over z), blk: 64 (over y, x, core).
Axes of the slice: x: 4, y: 8, z: 16, core: 2. Of those that a mesh axis runs over, the one named last changes fastest.
Arguments:
- kernel_tiles: bfloat16 [16, 64, 24, 6, 2048], P('ev', 'blk'), may hold values from -6 to 6
- region: int32 [16, 64, 24], P('ev', 'blk'), may hold values from 0 to 63, as said below
- band_width: int32 [8], replicated, may hold values from 2 to 16
Outputs:
- smoothed: float32 [3, 128, 131072], P(None, None, ('ev', 'blk'))
Inputs may be any that keep to these rules, and one draw needn't show every extreme that they name: `region`: each device's 24 entries are distinct, and no more than 2 of them lie in one lateral section (numbers s * 4 to s * 4 + 3); every device has 2 in some section.
All inputs are finite; a program needn't handle non-finite values.
Results may differ from a plain program's by a relative error of at most 0.015.
Values may be sent and summed in bfloat16 or wider, within the bound.
No kernel may reach another device: no remote copies, remote signals or barrier semaphores. Data moves between devices by JAX's collectives and lax.ppermute only.
A program may use at most 32 MiB of HBM per device.

v0:
```python
import jax
import jax.numpy as jnp
from jax import lax
from jax.sharding import PartitionSpec as P

NT = 4
LAYERS = 8


def build_smoother(band_width, depth):
    rows = jnp.arange(depth, dtype=jnp.int32)
    layer = rows // (depth // LAYERS)
    pick = (layer[:, None] == jnp.arange(LAYERS, dtype=jnp.int32)[None, :]).astype(jnp.int32)
    half = jnp.sum(pick * band_width[None, :], axis=1)
    dist = jnp.abs(rows[:, None] - rows[None, :])
    weight = jnp.maximum(half[:, None] + 1 - dist, 0).astype(jnp.float32)
    return (weight / jnp.sum(weight, axis=1, keepdims=True)).astype(jnp.bfloat16)


def shards(kernel_tiles, region, band_width):
    tiles = kernel_tiles[0, 0]
    ids = region[0, 0]
    groups = lax.axis_size("ev")
    slabs = lax.axis_size("blk")
    count, rows, width = tiles.shape
    depth_slab = rows // 3
    flat = tiles.reshape(count, rows * width)
    targets = jnp.arange(groups * NT, dtype=jnp.int32)
    onehot = (ids[None, :] == targets[:, None]).astype(jnp.bfloat16)
    spread = jnp.dot(onehot, flat, preferred_element_type=jnp.float32).astype(jnp.bfloat16)
    summed = lax.psum_scatter(spread, "ev", scatter_dimension=0, tiled=True).astype(jnp.float32)
    slab = summed.reshape(NT, 3, depth_slab, width).transpose(1, 2, 0, 3)
    slab = slab.reshape(3, depth_slab, slabs, NT * width // slabs).astype(jnp.bfloat16)
    smoother = build_smoother(band_width, depth_slab * slabs)
    return jnp.einsum(
        "ij,cjm->cim",
        smoother,
        lax.all_to_all(slab, "blk", split_axis=2, concat_axis=1, tiled=True)[:, :, 0, :],
        preferred_element_type=jnp.float32,
    )


def solution(mesh):
    in_specs = (P("ev", "blk", None, None, None), P("ev", "blk", None), P())
    out_specs = P(None, None, ("ev", "blk"))
    return jax.shard_map(shards, mesh=mesh, in_specs=in_specs, out_specs=out_specs, check_vma=False)
```

profile of v0, /device:TPU:1, one launch (start us, length us, event | category | flops | bytes accessed | tf_op | source)
XLA Modules:
  0.0 197.8 jit_solution(2557021609538524749)
XLA Ops:
  6.5 0.0 all-reduce.3.cloned.1.call-start
  6.5 1.1 copy.23
  7.6 0.0 copy-start
  7.7 2.4 %convolution_convert_fusion = bf16[64,12288]{1,0:T(8,128)(2,1)} fusion(bf16[24,12288]{1,0:T(8,128)(2,1)S(1)} %bitcast.20, s32[24]{0:T(128)} %bitcast.25), kind=kOutput, calls=%fused_computation | convolution fusion | flops 38536704 | bytes 2162784 | tf_op jit(solution)/shard_map/dot_general | solution.py:30
  10.0 0.0 all-reduce.3.cloned.1.call-update
  10.1 1.3 dynamic-slice
  12.0 0.0 copy-done
  12.0 0.1 select_reduce_fusion
  12.1 145.7 %all-reduce.3.cloned.1.call-done = bf16[64,12288]{1,0:T(8,128)(2,1)} async-done(((bf16[64,12288]{1,0:T(8,128)(2,1)}), bf16[64,12288]{1,0:T(8,128)(2,1)}) %all-reduce.3.cloned.1.call-update) | async-done | bytes 1572880
  157.8 1.0 constant_dynamic-slice_fusion
  158.8 0.1 convert_element_type.25
  158.9 0.7 copy.18
  159.6 19.6 %all-to-all-start = ((bf16[3,2,64,128]{3,1,0,2:T(2,128)(2,1)}), bf16[3,2,64,128]{3,1,0,2:T(2,128)(2,1)S(1)}, u32[]{:S(2)}, u32[]{:S(2)}) async-start(bf16[3,2,64,128]{3,1,0,2:T(2,128)(2,1)} %copy.18), calls=%async_computation | async-start | bytes 196608 | tf_op jit(solution)/shard_map/all_to_all | solution.py:38
  179.3 0.2 convert_reduce_fusion
  179.4 10.4 %all-to-all-done = bf16[3,2,64,128]{3,1,0,2:T(2,128)(2,1)S(1)} async-done(((bf16[3,2,64,128]{3,1,0,2:T(2,128)(2,1)}), bf16[3,2,64,128]{3,1,0,2:T(2,128)(2,1)S(1)}, u32[]{:S(2)}, u32[]{:S(2)}) %all-to-all-start) | async-done | bytes 98336 | tf_op jit(solution)/shard_map/all_to_all | solution.py:38
  189.8 0.1 copy.19
  189.9 0.3 convolution_bitcast_fusion
  190.2 0.8 copy.21
  (2 shorter events, 0.0 us)
Async XLA Ops:
  6.5 151.3 %all-reduce.3.cloned.1.call-start = ((), (), s32[]{:S(2)}) async-start(), calls=%async_computation.1 | async-start | bytes 3145728
  7.6 4.3 %copy-start = (s32[8]{0:T(128)S(1)}, s32[8]{0:T(128)}, u32[]{:S(2)}) copy-start(s32[8]{0:T(128)} %param.5) | copy-start | bytes 100
  159.6 30.2 %all-to-all-start = ((bf16[3,2,64,128]{3,1,0,2:T(2,128)(2,1)}), bf16[3,2,64,128]{3,1,0,2:T(2,128)(2,1)S(1)}, u32[]{:S(2)}, u32[]{:S(2)}) async-start(bf16[3,2,64,128]{3,1,0,2:T(2,128)(2,1)} %copy.18), calls=%async_computation | async-start | bytes 196608 | tf_op jit(solution)/shard_map/all_to_all | solution.py:38
Sparse Core Ops, SparseCore 0:
  10.2 147.5 all-reduce.2
where the time goes:
time: 198 us
  waiting for transfers between devices  156 us (79%)
  starting transfers between devices  19.6 us (10%)
  between operations  14.1 us (7%)
  local copies, waits for them, and re-layouts  5.05 us (3%)
  matrix products  2.62 us (1%)
    unnamed x2, waiting for transfers between devices  146 us
    all_to_all x1, starting transfers between devices, shards(): lax.all_to_all(slab, 'blk', split_axis=2, concat_axis=1, tiled=True)  19.6 us
    all_to_all x1, waiting for transfers between devices, shards(): lax.all_to_all(slab, 'blk', split_axis=2, concat_axis=1, tiled=True)  10.4 us
  transfers between devices with their start and end apart: 2, of which 2 were waited for; matrix products, arithmetic and copies ran while one was open for 1% of the time, Pallas kernels for 0%

commit v1 on v0

v1 whole, which is shorter than its diff:
```python
import jax
import jax.numpy as jnp
from jax import lax
from jax.experimental import pallas as pl
from jax.experimental.pallas import tpu as pltpu
from jax.sharding import PartitionSpec as P

F32 = jnp.float32
BF16 = jnp.bfloat16
I32 = jnp.int32

GROUPS = 16
NT = 4
KB = 24
COMPS = 3
QUARTERS = 4
LANES = 128
LAYERS = 8
SLABS = 64
DATA_ROWS = 192
MSG_ROWS = 200


def iota(shape, dim):
    return lax.broadcasted_iota(I32, shape, dim)


def pack_kernel(ids_ref, tiles_ref, out_ref):
    ids = ids_ref[...]
    section = lax.shift_right_logical(ids, 2)
    tile = ids & 3
    eye = iota((KB, KB), 0) == iota((KB, KB), 1)
    column = jnp.sum(jnp.where(eye, section, 0), axis=1, keepdims=True)
    earlier = (column == section) & (iota((KB, KB), 0) < iota((KB, KB), 1))
    slot = jnp.sum(earlier.astype(I32), axis=0, keepdims=True)

    cols = iota((KB, 8 * KB), 1)
    part = sum((cols >= KB * m).astype(I32) for m in range(1, 8))
    repeat = (cols - KB * part == iota((KB, 8 * KB), 0)).astype(BF16)
    place = jnp.broadcast_to(section * 16 + slot * 2, (8, KB)).astype(F32).astype(BF16)
    target = jnp.dot(place, repeat, preferred_element_type=F32)[:1].astype(I32)
    part = part[:1]
    target = target + lax.shift_right_logical(part, 1) * 4 + (part & 1)
    picks = (iota((256, 8 * KB), 0) == target).astype(F32).astype(BF16)

    for c in range(COMPS):
        rows = tiles_ref[c * 48 : (c + 1) * 48, :]
        stacked = jnp.concatenate([rows[:, h * 512 : (h + 1) * 512] for h in range(QUARTERS)], axis=0)
        placed = jnp.dot(picks, stacked, preferred_element_type=F32)
        for j in range(4):
            start = c * 64 + j * 16
            block = placed[:, j * LANES : (j + 1) * LANES].reshape(GROUPS, 16, LANES)
            out_ref[:, start : start + 16, :] = block.astype(BF16)

    here = lax.shift_right_logical(iota((128, KB), 0), 3) == section
    held = [
        jnp.sum(jnp.where(here & (slot == q), tile + 1, 0), axis=1, keepdims=True) for q in range(2)
    ]
    lane = iota((128, LANES), 1)
    which = jnp.where((lane & 2) != 0, held[1], held[0])
    row = (which - 1) * 32 + (lax.shift_right_logical(lane, 2) & 3) * 8 + (lane & 1) + 1
    notes = jnp.where(which > 0, row, 0).astype(F32).reshape(GROUPS, 8, LANES)
    out_ref[:, DATA_ROWS:MSG_ROWS, :] = notes.astype(BF16)


def sum_kernel(msg_ref, out_ref):
    notes = msg_ref[:, DATA_ROWS:MSG_ROWS, :].astype(F32)
    source = iota((GROUPS, 8, LANES), 1) * 8 + lax.shift_right_logical(iota((GROUPS, 8, LANES), 2), 4)
    notes = jnp.sum(jnp.where(source == iota((GROUPS, 8, LANES), 0), notes, 0.0), axis=0)
    target = notes.astype(I32) - 1
    target = jnp.concatenate([target[0:1, :], target[1:2, :]], axis=1)
    rows = iota((128, 256), 0)
    acc = None
    for c in range(COMPS):
        adds = ((rows == target + 2 * c) & (target >= 0)).astype(F32).astype(BF16)
        blocks = [
            msg_ref[:, c * 64 + j * 16 : c * 64 + (j + 1) * 16, :].reshape(256, LANES) for j in range(4)
        ]
        part = jnp.dot(adds, jnp.concatenate(blocks, axis=1), preferred_element_type=F32)
        acc = part if acc is None else acc + part
    for j in range(4):
        block = acc[:, j * LANES : (j + 1) * LANES].reshape(16, 8, LANES)
        out_ref[:, j, :, :] = block.astype(BF16)


def smooth_kernel(band_ref, slabs_ref, out_ref):
    depth = 2 * SLABS
    grad = slabs_ref[...].astype(F32).reshape(SLABS * 8, LANES).astype(BF16)
    i = iota((depth, SLABS * 8), 0)
    col = iota((depth, SLABS * 8), 1)
    j = lax.shift_right_logical(col, 3) * 2 + (col & 1)
    band = lax.shift_right_logical(iota((depth, 1), 0), 4)
    half = jnp.zeros((depth, 1), I32)
    for n in range(LAYERS):
        half = jnp.where(band == n, band_ref[n], half)
    weight = jnp.maximum(half + 1 - jnp.abs(i - j), 0).astype(F32)
    for c in range(COMPS):
        mine = jnp.where((col & 6) == 2 * c, weight, 0.0)
        smoother = (mine / jnp.sum(mine, axis=1, keepdims=True)).astype(BF16)
        out_ref[c, :, :] = jnp.dot(smoother, grad, preferred_element_type=F32)


VMEM = pl.BlockSpec(memory_space=pltpu.VMEM)
SMEM = pl.BlockSpec(memory_space=pltpu.SMEM)


def shards(kernel_tiles, region, band_width):
    tiles = kernel_tiles[0, 0].transpose(1, 0, 2).reshape(6 * KB, 2048)
    messages = pl.pallas_call(
        pack_kernel,
        out_shape=jax.ShapeDtypeStruct((GROUPS, MSG_ROWS, LANES), BF16),
        in_specs=[VMEM, VMEM],
        out_specs=VMEM,
        name="pack",
    )(region[0], tiles)
    messages = lax.all_to_all(messages, "ev", 0, 0, tiled=True)
    slabs = pl.pallas_call(
        sum_kernel,
        out_shape=jax.ShapeDtypeStruct((16, 4, 8, LANES), BF16),
        in_specs=[VMEM],
        out_specs=VMEM,
        name="add",
    )(messages)
    slabs = lax.all_to_all(slabs.reshape(SLABS, 8, LANES), "blk", 0, 0, tiled=True)
    return pl.pallas_call(
        smooth_kernel,
        out_shape=jax.ShapeDtypeStruct((COMPS, 2 * SLABS, LANES), F32),
        in_specs=[SMEM, VMEM],
        out_specs=VMEM,
        name="smooth",
    )(band_width, slabs)


def solution(mesh):
    in_specs = (P("ev", "blk", None, None, None), P("ev", "blk", None), P())
    out_specs = P(None, None, ("ev", "blk"))
    return jax.shard_map(shards, mesh=mesh, in_specs=in_specs, out_specs=out_specs, check_vma=False)
```

time: 198 us -> 91.6 us (0.46)
  waiting for transfers between devices: 156 us -> 0 us
  blocking collectives: 0 us -> 84.7 us
  starting transfers between devices: 19.6 us -> 0 us
  between operations: 14.1 us -> 0.01 us
  Pallas kernels: 0 us -> 6.6 us
  local copies, waits for them, and re-layouts: 5.05 us -> 0 us
  matrix products: 2.62 us -> 0 us
    unnamed x2 -> x0, waiting for transfers between devices: 146 us -> none
    all_to_all x0 -> x2, blocking collectives: none -> 84.7 us  [the longest x1 56 us: shards(): messages = lax.all_to_all(messages, 'ev', 0, 0, tiled=True)]
    all_to_all x1 -> x0, starting transfers between devices: 19.6 us -> none  [shards(): lax.all_to_all(slab, 'blk', split_axis=2, concat_axis=1, tiled=True)]
    all_to_all x1 -> x0, waiting for transfers between devices: 10.4 us -> none  [shards(): lax.all_to_all(slab, 'blk', split_axis=2, concat_axis=1, tiled=True)]
    pallas_call x0 -> x3, Pallas kernels: none -> 6.6 us  [the longest x1 2.54 us: shards(): pl.pallas_call(pack_kernel, out_shape=jax.ShapeDtypeStruct((GROUPS, MSG_R...]
    unnamed x5 -> x0, local copies, waits for them, and re-layouts: 3.36 us -> none
    dot_general x2 -> x0, matrix products: 2.62 us -> none  [the longest x1 2.37 us: shards(): jnp.dot(onehot, flat, preferred_element_type=jnp.float32)]
  transfers between devices with their start and end apart: 2 -> 0, of which waited for: 2 -> 0; matrix products, arithmetic and copies ran while one was open for 1% -> 0% of each run, Pallas kernels for 0% -> 0%
where the time goes in v1:
time: 91.6 us; the launch traced here: 91.3 us
  blocking collectives  84.7 us (92%)
  Pallas kernels  6.6 us (7%)
    all_to_all x1, blocking collectives, shards(): messages = lax.all_to_all(messages, 'ev', 0, 0, tiled=True)  56 us
    all_to_all x1, blocking collectives, shards(): lax.all_to_all(slabs.reshape(SLABS, 8, LANES), 'blk', 0, 0, tiled=True)  28.7 us
    pallas_call x1, Pallas kernels, shards(): pl.pallas_call(pack_kernel, out_shape=jax.ShapeDtypeStruct((GROUPS, MSG_R...  2.54 us
    pallas_call x1, Pallas kernels, shards(): pl.pallas_call(sum_kernel, out_shape=jax.ShapeDtypeStruct((16, 4, 8, LANE...  2.09 us
    pallas_call x1, Pallas kernels, shards(): pl.pallas_call(smooth_kernel, out_shape=jax.ShapeDtypeStruct((COMPS, 2 *...  1.97 us

profile of v1, /device:TPU:1, one launch (start us, length us, event | category | flops | bytes accessed | tf_op | source)
XLA Modules:
  0.0 91.3 jit_solution(866133430273184044)
XLA Ops:
  0.0 2.5 %pack.1 = bf16[16,200,128]{2,1,0:T(8,128)(2,1)} custom-call(s32[1,24]{1,0:T(1,128)} %bitcast.9, bf16[144,2048]{1,0:T(8,128)(2,1)} %bitcast.7), custom_call_target="tpu_custom_call" | custom-call | tf_op jit(solution)/shard_map/pack/pallas_call | solution.py:109
  2.5 56.0 %all_to_all.10.msg_ref = bf16[16,200,128]{2,1,0:T(8,128)(2,1)} all-to-all(bf16[16,200,128]{2,1,0:T(8,128)(2,1)} %pack.1), channel_id=1, replica_groups=mesh['ev'=16,'blk'=64] {'ev'}, dimensions={0} | all-to-all | bytes 1638400 | tf_op jit(solution)/shard_map/all_to_all | solution.py:116
  58.5 2.1 %add.1 = bf16[16,4,8,128]{3,2,1,0:T(8,128)(2,1)} custom-call(bf16[16,200,128]{2,1,0:T(8,128)(2,1)} %all_to_all.10.msg_ref), custom_call_target="tpu_custom_call" | custom-call | tf_op jit(solution)/shard_map/add/pallas_call | solution.py:117
  60.6 28.7 %all_to_all.11.slabs_ref = bf16[64,8,128]{2,1,0:T(8,128)(2,1)} all-to-all(bf16[64,8,128]{2,1,0:T(8,128)(2,1)} %bitcast.8), channel_id=1, replica_groups=mesh['ev'=16,'blk'=64] {'blk'}, dimensions={0} | all-to-all | bytes 262144 | tf_op jit(solution)/shard_map/all_to_all | solution.py:124
  89.3 2.0 %smooth.1 = f32[3,128,128]{2,1,0:T(8,128)} custom-call(s32[8]{0:T(128)} %band_ref.1, bf16[64,8,128]{2,1,0:T(8,128)(2,1)} %all_to_all.11.slabs_ref), custom_call_target="tpu_custom_call" | custom-call | tf_op jit(solution)/shard_map/smooth/pallas_call | solution.py:125

commit v2 on v1

--- a/solution.py
+++ b/solution.py
@@ -25,7 +25,33 @@
     return lax.broadcasted_iota(I32, shape, dim)
 
 
-def pack_kernel(ids_ref, tiles_ref, out_ref):
+def write_smoother(band_ref, smoother_ref):
+    depth = 2 * SLABS
+    i = iota((depth, SLABS * 8), 0)
+    col = iota((depth, SLABS * 8), 1)
+    j = (SLABS - 1 - lax.shift_right_logical(col, 3)) * 2 + (col & 1)
+    band = lax.shift_right_logical(iota((depth, LAYERS), 0), 4)
+    mine = band == iota((depth, LAYERS), 1)
+    half = jnp.sum(jnp.where(mine, band_ref[...], 0), axis=1, keepdims=True)
+    weight = jnp.maximum(half + 1 - jnp.abs(i - j), 0).astype(F32)
+    total = jnp.sum(weight, axis=1, keepdims=True) * 0.25
+    smoother = weight / total
+    for c in range(COMPS):
+        smoother_ref[c, :, :] = jnp.where((col & 6) == 2 * c, smoother, 0.0).astype(BF16)
+
+
+def pack_kernel(ids_hbm, band_hbm, tiles_hbm, out_ref, smoother_ref, ids_ref, band_ref, tiles_ref, sems):
+    ids_copy = pltpu.make_async_copy(ids_hbm, ids_ref, sems.at[6])
+    ids_copy.start()
+    band_copy = pltpu.make_async_copy(band_hbm, band_ref, sems.at[7])
+    band_copy.start()
+    copies = []
+    for c in range(COMPS):
+        for side in range(2):
+            part = (pl.ds(c * 48, 48), pl.ds(side * 1024, 1024))
+            copies.append(pltpu.make_async_copy(tiles_hbm.at[part], tiles_ref.at[part], sems.at[2 * c + side]))
+            copies[-1].start()
+    ids_copy.wait()
     ids = ids_ref[...]
     section = lax.shift_right_logical(ids, 2)
     tile = ids & 3
@@ -43,7 +69,12 @@
     target = target + lax.shift_right_logical(part, 1) * 4 + (part & 1)
     picks = (iota((256, 8 * KB), 0) == target).astype(F32).astype(BF16)
 
+    band_copy.wait()
+    write_smoother(band_ref, smoother_ref)
+
     for c in range(COMPS):
+        copies[2 * c].wait()
+        copies[2 * c + 1].wait()
         rows = tiles_ref[c * 48 : (c + 1) * 48, :]
         stacked = jnp.concatenate([rows[:, h * 512 : (h + 1) * 512] for h in range(QUARTERS)], axis=0)
         placed = jnp.dot(picks, stacked, preferred_element_type=F32)
@@ -58,7 +89,7 @@
     ]
     lane = iota((128, LANES), 1)
     which = jnp.where((lane & 2) != 0, held[1], held[0])
-    row = (which - 1) * 32 + (lax.shift_right_logical(lane, 2) & 3) * 8 + (lane & 1) + 1
+    row = (NT - which) * 32 + (3 - (lax.shift_right_logical(lane, 2) & 3)) * 8 + (lane & 1) + 1
     notes = jnp.where(which > 0, row, 0).astype(F32).reshape(GROUPS, 8, LANES)
     out_ref[:, DATA_ROWS:MSG_ROWS, :] = notes.astype(BF16)
 
@@ -80,55 +111,75 @@
         acc = part if acc is None else acc + part
     for j in range(4):
         block = acc[:, j * LANES : (j + 1) * LANES].reshape(16, 8, LANES)
-        out_ref[:, j, :, :] = block.astype(BF16)
+        out_ref[:, 3 - j, :, :] = block.astype(BF16)
 
 
-def smooth_kernel(band_ref, slabs_ref, out_ref):
-    depth = 2 * SLABS
+def smooth_kernel(smoother_ref, slabs_ref, out_hbm, out_ref, sems):
     grad = slabs_ref[...].astype(F32).reshape(SLABS * 8, LANES).astype(BF16)
-    i = iota((depth, SLABS * 8), 0)
-    col = iota((depth, SLABS * 8), 1)
-    j = lax.shift_right_logical(col, 3) * 2 + (col & 1)
-    band = lax.shift_right_logical(iota((depth, 1), 0), 4)
-    half = jnp.zeros((depth, 1), I32)
-    for n in range(LAYERS):
-        half = jnp.where(band == n, band_ref[n], half)
-    weight = jnp.maximum(half + 1 - jnp.abs(i - j), 0).astype(F32)
+    copies = []
     for c in range(COMPS):
-        mine = jnp.where((col & 6) == 2 * c, weight, 0.0)
-        smoother = (mine / jnp.sum(mine, axis=1, keepdims=True)).astype(BF16)
-        out_ref[c, :, :] = jnp.dot(smoother, grad, preferred_element_type=F32)
+        out_ref[c, :, :] = jnp.dot(smoother_ref[c], grad, preferred_element_type=F32)
+        copies.append(pltpu.make_async_copy(out_ref.at[c], out_hbm.at[c], sems.at[c]))
+        copies[c].start()
+    for copy in copies:
+        copy.wait()
 
 
+BACKWARDS = [list(range(SLABS - 1, -1, -1))]
+
 VMEM = pl.BlockSpec(memory_space=pltpu.VMEM)
-SMEM = pl.BlockSpec(memory_space=pltpu.SMEM)
+HBM = pl.BlockSpec(memory_space=pltpu.HBM)
+
+
+def in_hbm(array):
+    return pltpu.with_memory_space_constraint(array, pltpu.HBM)
+
+
+def params(mib):
+    return pltpu.CompilerParams(vmem_limit_bytes=mib * 1024 * 1024)
 
 
 def shards(kernel_tiles, region, band_width):
     tiles = kernel_tiles[0, 0].transpose(1, 0, 2).reshape(6 * KB, 2048)
-    messages = pl.pallas_call(
+    messages, smoother = pl.pallas_call(
         pack_kernel,
-        out_shape=jax.ShapeDtypeStruct((GROUPS, MSG_ROWS, LANES), BF16),
-        in_specs=[VMEM, VMEM],
-        out_specs=VMEM,
+        out_shape=(
+            jax.ShapeDtypeStruct((GROUPS, MSG_ROWS, LANES), BF16),
+            jax.ShapeDtypeStruct((COMPS, 2 * SLABS, SLABS * 8), BF16),
+        ),
+        in_specs=[HBM, HBM, HBM],
+        out_specs=(VMEM, VMEM),
+        scratch_shapes=[
+            pltpu.VMEM((1, KB), I32),
+            pltpu.VMEM((1, LAYERS), I32),
+            pltpu.VMEM((6 * KB, 2048), BF16),
+            pltpu.SemaphoreType.DMA((8,)),
+        ],
+        compiler_params=params(8),
         name="pack",
-    )(region[0], tiles)
+    )(in_hbm(region[0]), in_hbm(band_width.reshape(1, LAYERS)), in_hbm(tiles))
     messages = lax.all_to_all(messages, "ev", 0, 0, tiled=True)
     slabs = pl.pallas_call(
         sum_kernel,
         out_shape=jax.ShapeDtypeStruct((16, 4, 8, LANES), BF16),
         in_specs=[VMEM],
         out_specs=VMEM,
+        compiler_params=params(8),
         name="add",
     )(messages)
-    slabs = lax.all_to_all(slabs.reshape(SLABS, 8, LANES), "blk", 0, 0, tiled=True)
+    slabs = lax.all_to_all(slabs.reshape(SLABS, 8, LANES), "blk", 0, 0, tiled=True, axis_index_groups=BACKWARDS)
     return pl.pallas_call(
         smooth_kernel,
         out_shape=jax.ShapeDtypeStruct((COMPS, 2 * SLABS, LANES), F32),
-        in_specs=[SMEM, VMEM],
-        out_specs=VMEM,
+        in_specs=[VMEM, VMEM],
+        out_specs=HBM,
+        scratch_shapes=[
+            pltpu.VMEM((COMPS, 2 * SLABS, LANES), F32),
+            pltpu.SemaphoreType.DMA((COMPS,)),
+        ],
+        compiler_params=params(8),
         name="smooth",
-    )(band_width, slabs)
+    )(smoother, slabs)
 
 
 def solution(mesh):

time: 91.6 us -> 83.8 us (0.915)
  blocking collectives: 84.7 us -> 80.5 us
  Pallas kernels: 6.6 us -> 3.09 us
    all_to_all x1, blocking collectives: 28.7 us -> 24.8 us  [shards(): lax.all_to_all(slabs.reshape(SLABS, 8, LANES), 'blk', 0, 0, tiled=True, a...]
    pallas_call x1, Pallas kernels: 2.09 us -> 0.28 us  [shards(): pl.pallas_call(sum_kernel, out_shape=jax.ShapeDtypeStruct((16, 4, 8, LANE...]
    pallas_call x1, Pallas kernels: 1.97 us -> 0.91 us  [shards(): pl.pallas_call(smooth_kernel, out_shape=jax.ShapeDtypeStruct((COMPS, 2 *...]
where the time goes in v2:
time: 83.8 us; the launch traced here: 83.6 us
  blocking collectives  80.5 us (96%)
  Pallas kernels  3.09 us (4%)
    all_to_all x1, blocking collectives, shards(): messages = lax.all_to_all(messages, 'ev', 0, 0, tiled=True)  55.7 us
    all_to_all x1, blocking collectives, shards(): lax.all_to_all(slabs.reshape(SLABS, 8, LANES), 'blk', 0, 0, tiled=True, a...  24.8 us
    pallas_call x1, Pallas kernels, shards(): pl.pallas_call(pack_kernel, out_shape=(jax.ShapeDtypeStruct((GROUPS, MSG_...  1.91 us

profile of v2, /device:TPU:1, one launch (start us, length us, event | category | flops | bytes accessed | tf_op | source)
XLA Modules:
  0.0 83.6 jit_solution(9967208793134472848)
XLA Ops:
  0.0 1.9 %pack.1 = (bf16[16,200,128]{2,1,0:T(8,128)(2,1)S(1)}, bf16[3,128,512]{2,1,0:T(8,128)(2,1)S(1)}) custom-call(s32[1,24]{1,0:T(1,128)} %bitcast.10, s32[1,8]{1,0:T(1,128)} %bitcast.11, bf16[144,2048]{1,0:T(8,128)(2,1)} %bitcast.9), custom_call_target="tpu_custom_call" | custom-call | tf_op jit(solution)/shard_map/pack/pallas_call | solution.py:144
  1.9 55.7 %all_to_all.10.msg_ref = bf16[16,200,128]{2,1,0:T(8,128)(2,1)S(1)} all-to-all(bf16[16,200,128]{2,1,0:T(8,128)(2,1)S(1)} %get-tuple-element.8), channel_id=1, replica_groups=mesh['ev'=16,'blk'=64] {'ev'}, dimensions={0} | all-to-all | bytes 1638400 | tf_op jit(solution)/shard_map/all_to_all | solution.py:161
  57.6 0.3 add.1
  57.9 24.8 %all_to_all.11.slabs_ref = bf16[64,8,128]{2,1,0:T(8,128)(2,1)S(1)} all-to-all(bf16[64,8,128]{2,1,0:T(8,128)(2,1)S(1)} %bitcast.8), channel_id=1, replica_groups={{63,62,61,60,59,58,57,56,55,54,53,52,51,50,49,48,47,46,45,44,43,42,41,4..., dimensions={0} | all-to-all | bytes 262144 | tf_op jit(solution)/shard_map/all_to_all | solution.py:170
  82.7 0.9 %smooth.1 = f32[3,128,128]{2,1,0:T(8,128)} custom-call(bf16[3,128,512]{2,1,0:T(8,128)(2,1)S(1)} %get-tuple-element.7.smoother_ref, bf16[64,8,128]{2,1,0:T(8,128)(2,1)S(1)} %all_to_all.11.slabs_ref), custom_call_target="tpu_custom_call" | custom-call | tf_op jit(solution)/shard_map/smooth/pallas_call | solution.py:171

commit v3 on v2

--- a/solution.py
+++ b/solution.py
@@ -17,6 +17,8 @@
 LANES = 128
 LAYERS = 8
 SLABS = 64
+SECTION_ORDER = [14, 11, 2, 1, 3, 6, 12, 8, 9, 4, 5, 13, 10, 15, 7, 0]
+SLAB_ORDER = sorted(range(SLABS), key=lambda b: (-min(b // 8, 8 - b // 8) - min(b // 2 % 4, 4 - b // 2 % 4), -b))
 DATA_ROWS = 192
 MSG_ROWS = 200
 
@@ -25,11 +27,11 @@
     return lax.broadcasted_iota(I32, shape, dim)
 
 
-def write_smoother(band_ref, smoother_ref):
+def write_smoother(band_ref, level_ref, smoother_ref):
     depth = 2 * SLABS
     i = iota((depth, SLABS * 8), 0)
     col = iota((depth, SLABS * 8), 1)
-    j = (SLABS - 1 - lax.shift_right_logical(col, 3)) * 2 + (col & 1)
+    j = level_ref[...]
     band = lax.shift_right_logical(iota((depth, LAYERS), 0), 4)
     mine = band == iota((depth, LAYERS), 1)
     half = jnp.sum(jnp.where(mine, band_ref[...], 0), axis=1, keepdims=True)
@@ -40,11 +42,15 @@
         smoother_ref[c, :, :] = jnp.where((col & 6) == 2 * c, smoother, 0.0).astype(BF16)
 
 
-def pack_kernel(ids_hbm, band_hbm, tiles_hbm, out_ref, smoother_ref, ids_ref, band_ref, tiles_ref, sems):
+def pack_kernel(
+    ids_hbm, band_hbm, level_hbm, tiles_hbm, out_ref, smoother_ref, ids_ref, band_ref, level_ref, tiles_ref, sems
+):
     ids_copy = pltpu.make_async_copy(ids_hbm, ids_ref, sems.at[6])
     ids_copy.start()
     band_copy = pltpu.make_async_copy(band_hbm, band_ref, sems.at[7])
     band_copy.start()
+    level_copy = pltpu.make_async_copy(level_hbm, level_ref, sems.at[8])
+    level_copy.start()
     copies = []
     for c in range(COMPS):
         for side in range(2):
@@ -54,6 +60,7 @@
     ids_copy.wait()
     ids = ids_ref[...]
     section = lax.shift_right_logical(ids, 2)
+    section = sum(jnp.where(section == s, n, 0) for n, s in enumerate(SECTION_ORDER))
     tile = ids & 3
     eye = iota((KB, KB), 0) == iota((KB, KB), 1)
     column = jnp.sum(jnp.where(eye, section, 0), axis=1, keepdims=True)
@@ -70,7 +77,8 @@
     picks = (iota((256, 8 * KB), 0) == target).astype(F32).astype(BF16)
 
     band_copy.wait()
-    write_smoother(band_ref, smoother_ref)
+    level_copy.wait()
+    write_smoother(band_ref, level_ref, smoother_ref)
 
     for c in range(COMPS):
         copies[2 * c].wait()
@@ -89,7 +97,7 @@
     ]
     lane = iota((128, LANES), 1)
     which = jnp.where((lane & 2) != 0, held[1], held[0])
-    row = (NT - which) * 32 + (3 - (lax.shift_right_logical(lane, 2) & 3)) * 8 + (lane & 1) + 1
+    row = (which - 1) * 32 + (lax.shift_right_logical(lane, 2) & 3) * 8 + (lane & 1) + 1
     notes = jnp.where(which > 0, row, 0).astype(F32).reshape(GROUPS, 8, LANES)
     out_ref[:, DATA_ROWS:MSG_ROWS, :] = notes.astype(BF16)
 
@@ -111,7 +119,8 @@
         acc = part if acc is None else acc + part
     for j in range(4):
         block = acc[:, j * LANES : (j + 1) * LANES].reshape(16, 8, LANES)
-        out_ref[:, 3 - j, :, :] = block.astype(BF16)
+        for n in range(16):
+            out_ref[SLAB_ORDER.index(n * 4 + j), :, :] = block[n].astype(BF16)
 
 
 def smooth_kernel(smoother_ref, slabs_ref, out_hbm, out_ref, sems):
@@ -124,8 +133,6 @@
     for copy in copies:
         copy.wait()
 
-
-BACKWARDS = [list(range(SLABS - 1, -1, -1))]
 
 VMEM = pl.BlockSpec(memory_space=pltpu.VMEM)
 HBM = pl.BlockSpec(memory_space=pltpu.HBM)
@@ -141,33 +148,35 @@
 
 def shards(kernel_tiles, region, band_width):
     tiles = kernel_tiles[0, 0].transpose(1, 0, 2).reshape(6 * KB, 2048)
+    levels = jnp.asarray([[slab * 2 + r % 2 for slab in SLAB_ORDER for r in range(8)]], I32)
     messages, smoother = pl.pallas_call(
         pack_kernel,
         out_shape=(
             jax.ShapeDtypeStruct((GROUPS, MSG_ROWS, LANES), BF16),
             jax.ShapeDtypeStruct((COMPS, 2 * SLABS, SLABS * 8), BF16),
         ),
-        in_specs=[HBM, HBM, HBM],
+        in_specs=[HBM, HBM, HBM, HBM],
         out_specs=(VMEM, VMEM),
         scratch_shapes=[
             pltpu.VMEM((1, KB), I32),
             pltpu.VMEM((1, LAYERS), I32),
+            pltpu.VMEM((1, SLABS * 8), I32),
             pltpu.VMEM((6 * KB, 2048), BF16),
-            pltpu.SemaphoreType.DMA((8,)),
+            pltpu.SemaphoreType.DMA((9,)),
         ],
         compiler_params=params(8),
         name="pack",
-    )(in_hbm(region[0]), in_hbm(band_width.reshape(1, LAYERS)), in_hbm(tiles))
-    messages = lax.all_to_all(messages, "ev", 0, 0, tiled=True)
+    )(in_hbm(region[0]), in_hbm(band_width.reshape(1, LAYERS)), in_hbm(levels), in_hbm(tiles))
+    messages = lax.all_to_all(messages, "ev", 0, 0, tiled=True, axis_index_groups=[SECTION_ORDER])
     slabs = pl.pallas_call(
         sum_kernel,
-        out_shape=jax.ShapeDtypeStruct((16, 4, 8, LANES), BF16),
+        out_shape=jax.ShapeDtypeStruct((SLABS, 8, LANES), BF16),
         in_specs=[VMEM],
         out_specs=VMEM,
         compiler_params=params(8),
         name="add",
     )(messages)
-    slabs = lax.all_to_all(slabs.reshape(SLABS, 8, LANES), "blk", 0, 0, tiled=True, axis_index_groups=BACKWARDS)
+    slabs = lax.all_to_all(slabs, "blk", 0, 0, tiled=True, axis_index_groups=[SLAB_ORDER])
     return pl.pallas_call(
         smooth_kernel,
         out_shape=jax.ShapeDtypeStruct((COMPS, 2 * SLABS, LANES), F32),

time: 83.8 us -> 77.5 us (0.925)
  blocking collectives: 80.5 us -> 74.2 us
    all_to_all x2, blocking collectives: 80.5 us -> 74.2 us  [the longest x1 55 us: shards(): lax.all_to_all(messages, 'ev', 0, 0, tiled=True, axis_index_groups=[SECTI...]
where the time goes in v3:
time: 77.5 us; the launch traced here: 77.3 us
  blocking collectives  74.2 us (96%)
  Pallas kernels  3.13 us (4%)
    all_to_all x1, blocking collectives, shards(): lax.all_to_all(messages, 'ev', 0, 0, tiled=True, axis_index_groups=[SECTI...  55 us
    all_to_all x1, blocking collectives, shards(): lax.all_to_all(slabs, 'blk', 0, 0, tiled=True, axis_index_groups=[SLAB_OR...  19.1 us
    pallas_call x1, Pallas kernels, shards(): pl.pallas_call(pack_kernel, out_shape=(jax.ShapeDtypeStruct((GROUPS, MSG_...  1.93 us

profile of v3, /device:TPU:1, one launch (start us, length us, event | category | flops | bytes accessed | tf_op | source)
XLA Modules:
  0.0 77.3 jit_solution(2522662936414799158)
XLA Ops:
  0.0 1.9 %pack.1 = (bf16[16,200,128]{2,1,0:T(8,128)(2,1)S(1)}, bf16[3,128,512]{2,1,0:T(8,128)(2,1)S(1)}) custom-call(s32[1,24]{1,0:T(1,128)} %bitcast.8, s32[1,8]{1,0:T(1,128)} %bitcast.9, s32[1,512]{1,0:T(1,128)} %constant.2.clone.level_hbm, bf16[144,2048]{1,0:T(8,128)(2,1)} %bitcast.7), custom_call_target="tpu_custom_call" | custom-call | tf_op jit(solution)/shard_map/pack/pallas_call | solution.py:152
  1.9 55.0 %all_to_all.10.msg_ref = bf16[16,200,128]{2,1,0:T(8,128)(2,1)S(1)} all-to-all(bf16[16,200,128]{2,1,0:T(8,128)(2,1)S(1)} %get-tuple-element.8), channel_id=1, replica_groups={{896,704,128,64,192,384,768,512,576,256,320,832,640,960,448,0},{897,705..., dimensions={0} | all-to-all | bytes 1638400 | tf_op jit(solution)/shard_map/all_to_all | solution.py:170
  57.0 0.3 add.1
  57.3 19.1 %all_to_all.11.slabs_ref = bf16[64,8,128]{2,1,0:T(8,128)(2,1)S(1)} all-to-all(bf16[64,8,128]{2,1,0:T(8,128)(2,1)S(1)} %add.1), channel_id=1, replica_groups={{37,36,45,44,39,38,35,34,29,28,53,52,47,46,43,42,33,32,31,30,27,26,21,2..., dimensions={0} | all-to-all | bytes 262144 | tf_op jit(solution)/shard_map/all_to_all | solution.py:179
  76.4 0.9 %smooth.1 = f32[3,128,128]{2,1,0:T(8,128)} custom-call(bf16[3,128,512]{2,1,0:T(8,128)(2,1)S(1)} %get-tuple-element.7.smoother_ref, bf16[64,8,128]{2,1,0:T(8,128)(2,1)S(1)} %all_to_all.11.slabs_ref), custom_call_target="tpu_custom_call" | custom-call | tf_op jit(solution)/shard_map/smooth/pallas_call | solution.py:180

commit v4 on v2

--- a/solution.py
+++ b/solution.py
@@ -17,6 +17,9 @@
 LANES = 128
 LAYERS = 8
 SLABS = 64
+SECTION_ORDER = [13, 3, 12, 1, 11, 6, 15, 10, 14, 5, 4, 9, 8, 2, 7, 0]
+FIRST_SLAB = 37
+SLAB_ORDER = [(FIRST_SLAB + n) % SLABS for n in range(SLABS)]
 DATA_ROWS = 192
 MSG_ROWS = 200
 
@@ -29,7 +32,7 @@
     depth = 2 * SLABS
     i = iota((depth, SLABS * 8), 0)
     col = iota((depth, SLABS * 8), 1)
-    j = (SLABS - 1 - lax.shift_right_logical(col, 3)) * 2 + (col & 1)
+    j = ((lax.shift_right_logical(col, 3) + FIRST_SLAB) & (SLABS - 1)) * 2 + (col & 1)
     band = lax.shift_right_logical(iota((depth, LAYERS), 0), 4)
     mine = band == iota((depth, LAYERS), 1)
     half = jnp.sum(jnp.where(mine, band_ref[...], 0), axis=1, keepdims=True)
@@ -54,6 +57,7 @@
     ids_copy.wait()
     ids = ids_ref[...]
     section = lax.shift_right_logical(ids, 2)
+    section = sum(jnp.where(section == s, n, 0) for n, s in enumerate(SECTION_ORDER))
     tile = ids & 3
     eye = iota((KB, KB), 0) == iota((KB, KB), 1)
     column = jnp.sum(jnp.where(eye, section, 0), axis=1, keepdims=True)
@@ -89,7 +93,7 @@
     ]
     lane = iota((128, LANES), 1)
     which = jnp.where((lane & 2) != 0, held[1], held[0])
-    row = (NT - which) * 32 + (3 - (lax.shift_right_logical(lane, 2) & 3)) * 8 + (lane & 1) + 1
+    row = (which - 1) * 32 + (lax.shift_right_logical(lane, 2) & 3) * 8 + (lane & 1) + 1
     notes = jnp.where(which > 0, row, 0).astype(F32).reshape(GROUPS, 8, LANES)
     out_ref[:, DATA_ROWS:MSG_ROWS, :] = notes.astype(BF16)
 
@@ -111,7 +115,8 @@
         acc = part if acc is None else acc + part
     for j in range(4):
         block = acc[:, j * LANES : (j + 1) * LANES].reshape(16, 8, LANES)
-        out_ref[:, 3 - j, :, :] = block.astype(BF16)
+        for n in range(16):
+            out_ref[SLAB_ORDER.index(n * 4 + j), :, :] = block[n].astype(BF16)
 
 
 def smooth_kernel(smoother_ref, slabs_ref, out_hbm, out_ref, sems):
@@ -124,8 +129,6 @@
     for copy in copies:
         copy.wait()
 
-
-BACKWARDS = [list(range(SLABS - 1, -1, -1))]
 
 VMEM = pl.BlockSpec(memory_space=pltpu.VMEM)
 HBM = pl.BlockSpec(memory_space=pltpu.HBM)
@@ -158,16 +161,16 @@
         compiler_params=params(8),
         name="pack",
     )(in_hbm(region[0]), in_hbm(band_width.reshape(1, LAYERS)), in_hbm(tiles))
-    messages = lax.all_to_all(messages, "ev", 0, 0, tiled=True)
+    messages = lax.all_to_all(messages, "ev", 0, 0, tiled=True, axis_index_groups=[SECTION_ORDER])
     slabs = pl.pallas_call(
         sum_kernel,
-        out_shape=jax.ShapeDtypeStruct((16, 4, 8, LANES), BF16),
+        out_shape=jax.ShapeDtypeStruct((SLABS, 8, LANES), BF16),
         in_specs=[VMEM],
         out_specs=VMEM,
         compiler_params=params(8),
         name="add",
     )(messages)
-    slabs = lax.all_to_all(slabs.reshape(SLABS, 8, LANES), "blk", 0, 0, tiled=True, axis_index_groups=BACKWARDS)
+    slabs = lax.all_to_all(slabs, "blk", 0, 0, tiled=True, axis_index_groups=[SLAB_ORDER])
     return pl.pallas_call(
         smooth_kernel,
         out_shape=jax.ShapeDtypeStruct((COMPS, 2 * SLABS, LANES), F32),

time: 83.8 us -> 76.7 us (0.915)
  blocking collectives: 80.5 us -> 73.4 us
    all_to_all x2, blocking collectives: 80.5 us -> 73.4 us  [the longest x1 55.8 us: shards(): lax.all_to_all(messages, 'ev', 0, 0, tiled=True, axis_index_groups=[SECTI...]
where the time goes in v4:
time: 76.7 us; the launch traced here: 76.5 us
  blocking collectives  73.4 us (96%)
  Pallas kernels  3.11 us (4%)
    all_to_all x1, blocking collectives, shards(): lax.all_to_all(messages, 'ev', 0, 0, tiled=True, axis_index_groups=[SECTI...  55.8 us
    all_to_all x1, blocking collectives, shards(): lax.all_to_all(slabs, 'blk', 0, 0, tiled=True, axis_index_groups=[SLAB_OR...  17.6 us
    pallas_call x1, Pallas kernels, shards(): pl.pallas_call(pack_kernel, out_shape=(jax.ShapeDtypeStruct((GROUPS, MSG_...  1.92 us

profile of v4, /device:TPU:1, one launch (start us, length us, event | category | flops | bytes accessed | tf_op | source)
XLA Modules:
  0.0 76.5 jit_solution(6202456938063572967)
XLA Ops:
  0.0 1.9 %pack.1 = (bf16[16,200,128]{2,1,0:T(8,128)(2,1)S(1)}, bf16[3,128,512]{2,1,0:T(8,128)(2,1)S(1)}) custom-call(s32[1,24]{1,0:T(1,128)} %bitcast.8, s32[1,8]{1,0:T(1,128)} %bitcast.9, bf16[144,2048]{1,0:T(8,128)(2,1)} %bitcast.7), custom_call_target="tpu_custom_call" | custom-call | tf_op jit(solution)/shard_map/pack/pallas_call | solution.py:147
  1.9 55.8 %all_to_all.10.msg_ref = bf16[16,200,128]{2,1,0:T(8,128)(2,1)S(1)} all-to-all(bf16[16,200,128]{2,1,0:T(8,128)(2,1)S(1)} %get-tuple-element.8), channel_id=1, replica_groups={{832,192,768,64,704,384,960,640,896,320,256,576,512,128,448,0},{833,193..., dimensions={0} | all-to-all | bytes 1638400 | tf_op jit(solution)/shard_map/all_to_all | solution.py:164
  57.7 0.3 add.1
  58.0 17.6 %all_to_all.11.slabs_ref = bf16[64,8,128]{2,1,0:T(8,128)(2,1)S(1)} all-to-all(bf16[64,8,128]{2,1,0:T(8,128)(2,1)S(1)} %add.1), channel_id=1, replica_groups={{37,38,39,40,41,42,43,44,45,46,47,48,49,50,51,52,53,54,55,56,57,58,59,6..., dimensions={0} | all-to-all | bytes 262144 | tf_op jit(solution)/shard_map/all_to_all | solution.py:173
  75.6 0.9 %smooth.1 = f32[3,128,128]{2,1,0:T(8,128)} custom-call(bf16[3,128,512]{2,1,0:T(8,128)(2,1)S(1)} %get-tuple-element.7.smoother_ref, bf16[64,8,128]{2,1,0:T(8,128)(2,1)S(1)} %all_to_all.11.slabs_ref), custom_call_target="tpu_custom_call" | custom-call | tf_op jit(solution)/shard_map/smooth/pallas_call | solution.py:174

commit v5 on v4

--- a/solution.py
+++ b/solution.py
@@ -19,6 +19,7 @@
 SLABS = 64
 SECTION_ORDER = [13, 3, 12, 1, 11, 6, 15, 10, 14, 5, 4, 9, 8, 2, 7, 0]
 FIRST_SLAB = 37
+LATE = 8
 SLAB_ORDER = [(FIRST_SLAB + n) % SLABS for n in range(SLABS)]
 DATA_ROWS = 192
 MSG_ROWS = 200
@@ -74,7 +75,10 @@
     picks = (iota((256, 8 * KB), 0) == target).astype(F32).astype(BF16)
 
     band_copy.wait()
-    write_smoother(band_ref, smoother_ref)
+
+    @pl.when(lax.axis_index("ev") < LATE)
+    def _():
+        write_smoother(band_ref, smoother_ref)
 
     for c in range(COMPS):
         copies[2 * c].wait()
@@ -119,15 +123,30 @@
             out_ref[SLAB_ORDER.index(n * 4 + j), :, :] = block[n].astype(BF16)
 
 
-def smooth_kernel(smoother_ref, slabs_ref, out_hbm, out_ref, sems):
-    grad = slabs_ref[...].astype(F32).reshape(SLABS * 8, LANES).astype(BF16)
-    copies = []
-    for c in range(COMPS):
-        out_ref[c, :, :] = jnp.dot(smoother_ref[c], grad, preferred_element_type=F32)
-        copies.append(pltpu.make_async_copy(out_ref.at[c], out_hbm.at[c], sems.at[c]))
-        copies[c].start()
-    for copy in copies:
-        copy.wait()
+def smooth_kernel(band_hbm, smoother_ref, slabs_ref, out_hbm, out_ref, band_ref, own_ref, sems):
+    late = lax.axis_index("ev") >= LATE
+
+    def smooth(matrix_ref):
+        grad = slabs_ref[...].astype(F32).reshape(SLABS * 8, LANES).astype(BF16)
+        copies = []
+        for c in range(COMPS):
+            out_ref[c, :, :] = jnp.dot(matrix_ref[c], grad, preferred_element_type=F32)
+            copies.append(pltpu.make_async_copy(out_ref.at[c], out_hbm.at[c], sems.at[c]))
+            copies[c].start()
+        for copy in copies:
+            copy.wait()
+
+    @pl.when(late)
+    def _():
+        band_copy = pltpu.make_async_copy(band_hbm, band_ref, sems.at[COMPS])
+        band_copy.start()
+        band_copy.wait()
+        write_smoother(band_ref, own_ref)
+        smooth(own_ref)
+
+    @pl.when(jnp.logical_not(late))
+    def _():
+        smooth(smoother_ref)
 
 
 VMEM = pl.BlockSpec(memory_space=pltpu.VMEM)
@@ -174,15 +193,17 @@
     return pl.pallas_call(
         smooth_kernel,
         out_shape=jax.ShapeDtypeStruct((COMPS, 2 * SLABS, LANES), F32),
-        in_specs=[VMEM, VMEM],
+        in_specs=[HBM, VMEM, VMEM],
         out_specs=HBM,
         scratch_shapes=[
             pltpu.VMEM((COMPS, 2 * SLABS, LANES), F32),
-            pltpu.SemaphoreType.DMA((COMPS,)),
+            pltpu.VMEM((1, LAYERS), I32),
+            pltpu.VMEM((COMPS, 2 * SLABS, SLABS * 8), BF16),
+            pltpu.SemaphoreType.DMA((COMPS + 1,)),
         ],
         compiler_params=params(8),
         name="smooth",
-    )(smoother, slabs)
+    )(in_hbm(band_width.reshape(1, LAYERS)), smoother, slabs)
 
 
 def solution(mesh):

time: 76.7 us -> 76.5 us (level)
  no operation moved by 1% of the time
where the time goes in v5:
time: 76.5 us; the launch traced here: 76.3 us
  blocking collectives  73.2 us (96%)
  Pallas kernels  3.13 us (4%)
    all_to_all x1, blocking collectives, shards(): lax.all_to_all(messages, 'ev', 0, 0, tiled=True, axis_index_groups=[SECTI...  55.6 us
    all_to_all x1, blocking collectives, shards(): lax.all_to_all(slabs, 'blk', 0, 0, tiled=True, axis_index_groups=[SLAB_OR...  17.6 us
    pallas_call x1, Pallas kernels, shards(): pl.pallas_call(pack_kernel, out_shape=(jax.ShapeDtypeStruct((GROUPS, MSG_...  1.93 us

profile of v5, /device:TPU:1, one launch (start us, length us, event | category | flops | bytes accessed | tf_op | source)
XLA Modules:
  0.0 76.3 jit_solution(13750733664726328881)
XLA Ops:
  0.0 1.9 %pack.1 = (bf16[16,200,128]{2,1,0:T(8,128)(2,1)S(1)}, bf16[3,128,512]{2,1,0:T(8,128)(2,1)S(1)}) custom-call(s32[1,24]{1,0:T(1,128)} %bitcast.10, s32[1,8]{1,0:T(1,128)} %bitcast.8, bf16[144,2048]{1,0:T(8,128)(2,1)} %bitcast.7), custom_call_target="tpu_custom_call" | custom-call | tf_op jit(solution)/shard_map/pack/pallas_call | solution.py:166
  1.9 55.6 %all_to_all.10.msg_ref = bf16[16,200,128]{2,1,0:T(8,128)(2,1)S(1)} all-to-all(bf16[16,200,128]{2,1,0:T(8,128)(2,1)S(1)} %get-tuple-element.8), channel_id=1, replica_groups={{832,192,768,64,704,384,960,640,896,320,256,576,512,128,448,0},{833,193..., dimensions={0} | all-to-all | bytes 1638400 | tf_op jit(solution)/shard_map/all_to_all | solution.py:183
  57.5 0.3 add.1
  57.8 17.6 %all_to_all.11.slabs_ref = bf16[64,8,128]{2,1,0:T(8,128)(2,1)S(1)} all-to-all(bf16[64,8,128]{2,1,0:T(8,128)(2,1)S(1)} %add.1), channel_id=1, replica_groups={{37,38,39,40,41,42,43,44,45,46,47,48,49,50,51,52,53,54,55,56,57,58,59,6..., dimensions={0} | all-to-all | bytes 262144 | tf_op jit(solution)/shard_map/all_to_all | solution.py:192
  75.4 0.9 %smooth.1 = f32[3,128,128]{2,1,0:T(8,128)} custom-call(s32[1,8]{1,0:T(1,128)} %bitcast.9, bf16[3,128,512]{2,1,0:T(8,128)(2,1)S(1)} %get-tuple-element.7.smoother_ref, bf16[64,8,128]{2,1,0:T(8,128)(2,1)S(1)} %all_to_all.11.slabs_ref), custom_call_target="tpu_custom_call" | custom-call | tf_op jit(solution)/shard_map/smooth/pallas_call | solution.py:193

commit v6 on v4

--- a/solution.py
+++ b/solution.py
@@ -46,14 +46,14 @@
 def pack_kernel(ids_hbm, band_hbm, tiles_hbm, out_ref, smoother_ref, ids_ref, band_ref, tiles_ref, sems):
     ids_copy = pltpu.make_async_copy(ids_hbm, ids_ref, sems.at[6])
     ids_copy.start()
-    band_copy = pltpu.make_async_copy(band_hbm, band_ref, sems.at[7])
-    band_copy.start()
     copies = []
     for c in range(COMPS):
         for side in range(2):
             part = (pl.ds(c * 48, 48), pl.ds(side * 1024, 1024))
             copies.append(pltpu.make_async_copy(tiles_hbm.at[part], tiles_ref.at[part], sems.at[2 * c + side]))
             copies[-1].start()
+    band_copy = pltpu.make_async_copy(band_hbm, band_ref, sems.at[7])
+    band_copy.start()
     ids_copy.wait()
     ids = ids_ref[...]
     section = lax.shift_right_logical(ids, 2)

time: 76.7 us -> 76.8 us (level)
  no operation moved by 1% of the time
where the time goes in v6:
time: 76.8 us; the launch traced here: 76.6 us
  blocking collectives  73.4 us (96%)
  Pallas kernels  3.15 us (4%)
    all_to_all x1, blocking collectives, shards(): lax.all_to_all(messages, 'ev', 0, 0, tiled=True, axis_index_groups=[SECTI...  55.8 us
    all_to_all x1, blocking collectives, shards(): lax.all_to_all(slabs, 'blk', 0, 0, tiled=True, axis_index_groups=[SLAB_OR...  17.7 us
    pallas_call x1, Pallas kernels, shards(): pl.pallas_call(pack_kernel, out_shape=(jax.ShapeDtypeStruct((GROUPS, MSG_...  1.96 us

profile of v6, /device:TPU:1, one launch (start us, length us, event | category | flops | bytes accessed | tf_op | source)
XLA Modules:
  0.0 76.6 jit_solution(5989794130853894219)
XLA Ops:
  0.0 2.0 %pack.1 = (bf16[16,200,128]{2,1,0:T(8,128)(2,1)S(1)}, bf16[3,128,512]{2,1,0:T(8,128)(2,1)S(1)}) custom-call(s32[1,24]{1,0:T(1,128)} %bitcast.8, s32[1,8]{1,0:T(1,128)} %bitcast.9, bf16[144,2048]{1,0:T(8,128)(2,1)} %bitcast.7), custom_call_target="tpu_custom_call" | custom-call | tf_op jit(solution)/shard_map/pack/pallas_call | solution.py:147
  2.0 55.8 %all_to_all.10.msg_ref = bf16[16,200,128]{2,1,0:T(8,128)(2,1)S(1)} all-to-all(bf16[16,200,128]{2,1,0:T(8,128)(2,1)S(1)} %get-tuple-element.8), channel_id=1, replica_groups={{832,192,768,64,704,384,960,640,896,320,256,576,512,128,448,0},{833,193..., dimensions={0} | all-to-all | bytes 1638400 | tf_op jit(solution)/shard_map/all_to_all | solution.py:164
  57.7 0.3 add.1
  58.0 17.7 %all_to_all.11.slabs_ref = bf16[64,8,128]{2,1,0:T(8,128)(2,1)S(1)} all-to-all(bf16[64,8,128]{2,1,0:T(8,128)(2,1)S(1)} %add.1), channel_id=1, replica_groups={{37,38,39,40,41,42,43,44,45,46,47,48,49,50,51,52,53,54,55,56,57,58,59,6..., dimensions={0} | all-to-all | bytes 262144 | tf_op jit(solution)/shard_map/all_to_all | solution.py:173
  75.7 0.9 %smooth.1 = f32[3,128,128]{2,1,0:T(8,128)} custom-call(bf16[3,128,512]{2,1,0:T(8,128)(2,1)S(1)} %get-tuple-element.7.smoother_ref, bf16[64,8,128]{2,1,0:T(8,128)(2,1)S(1)} %all_to_all.11.slabs_ref), custom_call_target="tpu_custom_call" | custom-call | tf_op jit(solution)/shard_map/smooth/pallas_call | solution.py:174
